TPU v7x, 512 devices: a whole 4x8x8 slice. The times are simulated.
512 devices in a mesh: row: 16 (over y, x_lo), col: 16 (over x_hi, z), half: 2 (over core).
Axes of the slice: x: 4 (x_hi: 2, x_lo: 2; x = x_hi * 2 + x_lo), y: 8, z: 8, core: 2. Of those that a mesh axis runs over, the one named last changes fastest.
Arguments:
- frames: float32 [512, 16384], P('half', ('row', 'col')), as said below
Outputs:
- covariance: float32 [16384, 16384], P('row', ('col', 'half'))
Inputs may be any that keep to these rules, and one draw needn't show every extreme that they name: `frames`: positive intensities: a pixel background times a frame brightness times a rough factor.
All inputs are finite; a program needn't handle non-finite values.
Results may differ from a plain program's by a relative error of at most 0.00008.
Values sent between devices are 32-bit elements; how exact they have to be, the bound alone decides.
A program may use at most 64 MiB of HBM per device.

v0:
```python
import jax
import jax.numpy as jnp
from jax import lax
from jax.experimental import pallas as pl
from jax.experimental.pallas import tpu as pltpu
from jax.sharding import PartitionSpec as P

MESH = pl.DeviceIdType.MESH
FRAMES = 512
HALF = FRAMES // 2
RING = 8
TILE = 128


def mod8(value):
    return lax.rem(value + 16, RING)


def split(value):
    hi = value.astype(jnp.bfloat16)
    lo = (value - hi.astype(jnp.float32)).astype(jnp.bfloat16)
    return hi, lo


def kernel(stage, out_ref, traw, rows, cols, lhs, rhs,
           t_s, t_r, rx_s, rx_r, cx_s, cx_r, rr_s, rr_r, c_s, c_r, sib_s, sib_r):
    row = lax.axis_index("row")
    col = lax.axis_index("col")
    half = lax.axis_index("half")
    y, xl = row // 2, lax.rem(row, 2)
    xh, z = col // RING, lax.rem(col, RING)
    other = 1 - half

    sibling = (row, col, other)
    rx_peer = (row, (1 - xh) * RING + z, half)
    z_peer = {n: (row, xh * RING + mod8(z + n), half) for n in (1, -1, 2, -2)}
    cx_peer = (y * 2 + 1 - xl, col, half)
    y_peer = {n: (mod8(y + n) * 2 + xl, col, half) for n in (1, -1, 2, -2)}

    yy = mod8(z + lax.rem(row, RING) + 4 * xh)
    t_dest = [(yy * 2 + s, row, xh) for s in range(2)]
    t_self = [(yy * 2 + s == row) & (row == col) & (xh == half) for s in range(2)]

    def part(place):
        return mod8(place - z + 4 * half)

    t_col = RING * half + part(y)
    from_self = (row == col) & (col == t_col)

    barrier = pltpu.get_barrier_semaphore()
    for peer in (sibling, rx_peer, cx_peer, *z_peer.values(), *y_peer.values(), (col, t_col, other)):
        pl.semaphore_signal(barrier, inc=1, device_id=peer, device_id_type=MESH)

    @pl.when(jnp.logical_not(from_self))
    def _():
        pl.semaphore_signal(barrier, inc=1, device_id=(col, t_col, half), device_id_type=MESH)

    rows[half, col] = stage[...]
    pl.semaphore_wait(barrier, jnp.where(from_self, 12, 13))

    def remote(src, dst, send, recv, peer):
        return pltpu.make_async_remote_copy(
            src_ref=src, dst_ref=dst, send_sem=send, recv_sem=recv, device_id=peer, device_id_type=MESH)

    def arrived(ref, sem):
        pltpu.make_async_copy(ref, ref, sem).wait()

    pending = []

    def start(copy):
        copy.start()
        pending.append(copy)

    t_copies = []

    def transpose_out():
        for s in range(2):
            src = stage.at[pl.ds(s * 32, 32)]
            far = remote(src, traw.at[half], t_s.at[s], t_r.at[half], t_dest[s])
            near = pltpu.make_async_copy(src, traw.at[half], t_r.at[half])

            @pl.when(t_self[s])
            def _():
                near.start()

            @pl.when(jnp.logical_not(t_self[s]))
            def _():
                far.start()

            t_copies.append((t_self[s], far))

    def k_of(u, d):
        return (xh if u == 0 else 1 - xh) * RING + mod8(z + d)

    def row_ref(u, d):
        return rows.at[half, k_of(u, d)]

    def col_ref(u, d):
        return cols.at[part(mod8(y + d)), xl if u == 0 else 1 - xl]

    def hop(which, direction, step, u):
        behind, ahead = ((0, 1), (0, 2), (2, 1), (2, 2))[step - 1]
        at = (0 if direction == 1 else 1, step - 1, u)
        if which == "row":
            ref, send, recv, peer = row_ref(u, -direction * behind), rr_s, rr_r, z_peer[direction * ahead]
        else:
            ref, send, recv, peer = col_ref(u, -direction * behind), c_s, c_r, y_peer[direction * ahead]
        return remote(ref, ref, send.at[at], recv.at[at], peer)

    def sends(direction, step, u):
        return step < 4 or (direction == 1) == (u == 0)

    def slots(step, u):
        if step == 0:
            return ((u, 0),)
        if step == 4:
            return ((14 + u, 4),)
        return tuple((2 + (step - 1) * 4 + (0 if n == 1 else 2) + u, -n * step) for n in (1, -1))

    def to_sibling(slot, u, d):
        start(remote(row_ref(u, d), row_ref(u, d), sib_s.at[slot], sib_r.at[slot], sibling))

    def first_hops(which, u):
        for step in (2, 1):
            for direction in (1, -1):
                start(hop(which, direction, step, u))

    def begin_row(u):
        if u == 1:
            arrived(row_ref(1, 0), rx_r)
        first_hops("row", u)
        to_sibling(u, u, 0)

    def forward(which, step, u):
        n = 0
        for direction in (1, -1):
            if not sends(direction, step, u):
                continue
            slot, d = slots(step, u)[n]
            n += 1
            ref, recv = (row_ref(u, d), rr_r) if which == "row" else (col_ref(u, d), c_r)
            arrived(ref, recv.at[0 if direction == 1 else 1, step - 1, u])
            for later in (4, 3) if step == 2 else ():
                if sends(direction, later, u):
                    start(hop(which, direction, later, u))
            if which == "row":
                to_sibling(slot, u, d)

    def to_lhs(step, u):
        for slot, d in slots(step, u):
            k = k_of(u, d)
            arrived(rows.at[other, k], sib_r.at[slot])
            first, second = rows[0, k], rows[1, k]
            total = jnp.sum(first, axis=1, keepdims=True) + jnp.sum(second, axis=1, keepdims=True)
            mean = total / FRAMES
            here = pl.ds(pl.multiple_of(k * 64, 64), 64)
            for j, value in enumerate((first, second)):
                hi, lo = split(value - mean)
                lhs[here, j * HALF:(j + 1) * HALF] = hi
                lhs[here, FRAMES + j * HALF:FRAMES + (j + 1) * HALF] = lo
                lhs[here, 2 * FRAMES + j * HALF:2 * FRAMES + (j + 1) * HALF] = hi

    def begin_col(u):
        if u == 1:
            arrived(col_ref(1, 0), cx_r)
            first_hops("col", 1)
            return
        for g in range(2):
            arrived(traw.at[g], t_r.at[g])
        first, second = traw[0], traw[1]
        total = jnp.sum(first, axis=1, keepdims=True) + jnp.sum(second, axis=1, keepdims=True)
        mean = total / FRAMES
        mine = col_ref(0, 0)
        mine[:, :HALF] = first - mean
        mine[:, HALF:] = second - mean
        start(remote(mine, mine, cx_s, cx_r, cx_peer))
        first_hops("col", 0)

    base = part(y)
    sign = 1 - 2 * lax.rem(base, 2)

    def tile_of(step):
        return mod8(base + sign * (1, -2, 3, 4)[step - 1]) // 2

    def to_rhs(steps):
        for i, step in enumerate(steps):
            value = cols[pl.ds(2 * tile_of(step), 2)].reshape(TILE, FRAMES) * (1.0 / (FRAMES - 1))
            hi, lo = split(value)
            here = pl.ds(i * TILE, TILE)
            rhs[here, :FRAMES] = hi
            rhs[here, FRAMES:2 * FRAMES] = hi
            rhs[here, 2 * FRAMES:] = lo

    def multiply(steps, u):
        here = pl.ds(pl.multiple_of((xh if u == 0 else 1 - xh) * 512, 512), 512)
        product = lax.dot_general(
            lhs[here, :], rhs[...], (((1,), (1,)), ((), ())), preferred_element_type=jnp.float32)
        for i, step in enumerate(steps):
            there = pl.ds(pl.multiple_of(tile_of(step) * TILE, TILE), TILE)
            out_ref[here, there] = product[:, i * TILE:(i + 1) * TILE]

    transpose_out()
    start(remote(row_ref(0, 0), row_ref(0, 0), rx_s, rx_r, rx_peer))
    begin_row(0)
    begin_row(1)
    begin_col(0)
    forward("row", 2, 0)
    begin_col(1)
    forward("row", 2, 1)
    forward("col", 2, 0)
    forward("row", 1, 0)
    to_lhs(0, 0)
    to_lhs(0, 1)
    forward("col", 2, 1)
    forward("row", 1, 1)
    to_lhs(2, 0)
    forward("row", 3, 0)
    forward("row", 4, 0)
    to_lhs(1, 0)
    to_lhs(2, 1)
    to_lhs(1, 1)
    forward("row", 3, 1)
    forward("row", 4, 1)
    to_lhs(3, 0)
    to_lhs(4, 0)
    for u in range(2):
        forward("col", 1, u)
    to_rhs((1, 2))
    multiply((1, 2), 0)
    to_lhs(3, 1)
    to_lhs(4, 1)
    multiply((1, 2), 1)
    for u in range(2):
        forward("col", 3, u)
        forward("col", 4, u)
    to_rhs((3, 4))
    multiply((3, 4), 0)
    multiply((3, 4), 1)

    for copy in pending:
        copy.wait_send()
    for local, copy in t_copies:
        @pl.when(jnp.logical_not(local))
        def _():
            copy.wait_send()


def body(frames):
    dma = pltpu.SemaphoreType.DMA
    return pl.pallas_call(
        kernel,
        out_shape=jax.ShapeDtypeStruct((1024, 512), jnp.float32),
        in_specs=[pl.BlockSpec(memory_space=pltpu.VMEM)],
        out_specs=pl.BlockSpec(memory_space=pltpu.VMEM),
        scratch_shapes=[
            pltpu.VMEM((2, 32, HALF), jnp.float32),
            pltpu.VMEM((2, 16, 64, HALF), jnp.float32),
            pltpu.VMEM((8, 2, 32, FRAMES), jnp.float32),
            pltpu.VMEM((1024, 3 * FRAMES), jnp.bfloat16),
            pltpu.VMEM((2 * TILE, 3 * FRAMES), jnp.bfloat16),
            dma((2,)), dma((2,)), dma, dma, dma, dma, dma((2, 4, 2)), dma((2, 4, 2)), dma((2, 4, 2)), dma((2, 4, 2)),
            dma((16,)), dma((16,)),
        ],
        compiler_params=pltpu.CompilerParams(
            collective_id=0, has_side_effects=True, vmem_limit_bytes=40 * 1024 * 1024),
        cost_estimate=pl.CostEstimate(flops=3 * 2 * 1024 * 512 * 512, bytes_accessed=2 << 20, transcendentals=0),
    )(frames.T)


def solution(mesh):
    in_specs = (P("half", ("row", "col")),)
    out_specs = P("row", ("col", "half"))
    return jax.shard_map(body, mesh=mesh, in_specs=in_specs, out_specs=out_specs, check_vma=False)
```

profile of v0, /device:TPU:1, one launch (start us, length us, event | category | flops | bytes accessed | tf_op | source)
XLA Modules:
  0.0 39.8 jit_solution(8804830621702097974)
XLA Ops:
  0.0 0.0 copy-start
  0.0 0.8 %copy-done = f32[256,64]{0,1:T(8,128)S(1)} copy-done((f32[256,64]{0,1:T(8,128)S(1)}, f32[256,64]{0,1:T(8,128)}, u32[]{:S(2)}) %copy-start) | copy-done | bytes 65560
  0.8 37.7 %shard_map.17 = f32[1024,512]{1,0:T(8,128)S(1)} custom-call(f32[64,256]{1,0:T(8,128)S(1)} %bitcast.1), custom_call_target="tpu_custom_call" | custom-call | flops 1610612736 | bytes 2097152 | tf_op jit(solution)/shard_map/pallas_call | solution.py:250
  38.5 1.3 %copy.3 = f32[1024,512]{1,0:T(8,128)} copy(f32[1024,512]{1,0:T(8,128)S(1)} %shard_map.17) | data formatting | bytes 4194304
Async XLA Ops:
  0.0 0.8 %copy-start = (f32[256,64]{0,1:T(8,128)S(1)}, f32[256,64]{0,1:T(8,128)}, u32[]{:S(2)}) copy-start(f32[256,64]{0,1:T(8,128)} %param.1) | copy-start | bytes 196612
where the time goes:
time: 40.4 us; the launch traced here: 39.8 us
  Pallas kernels  37.7 us (93%)
  local copies, waits for them, and re-layouts  2.16 us (5%)
    pallas_call x1, Pallas kernels, body(): pl.pallas_call(kernel, out_shape=jax.ShapeDtypeStruct((1024, 512), jnp.fl...  37.7 us
    unnamed x3, local copies, waits for them, and re-layouts  2.16 us

commit v1 on v0

--- a/solution.py
+++ b/solution.py
@@ -36,6 +36,7 @@
     z_peer = {n: (row, xh * RING + mod8(z + n), half) for n in (1, -1, 2, -2)}
     cx_peer = (y * 2 + 1 - xl, col, half)
     y_peer = {n: (mod8(y + n) * 2 + xl, col, half) for n in (1, -1, 2, -2)}
+    diagonal = {n: (mod8(y + n) * 2 + 1 - xl, col, half) for n in (1, -1, 2, -2)}
 
     yy = mod8(z + lax.rem(row, RING) + 4 * xh)
     t_dest = [(yy * 2 + s, row, xh) for s in range(2)]
@@ -48,7 +49,7 @@
     from_self = (row == col) & (col == t_col)
 
     barrier = pltpu.get_barrier_semaphore()
-    for peer in (sibling, rx_peer, cx_peer, *z_peer.values(), *y_peer.values(), (col, t_col, other)):
+    for peer in (sibling, rx_peer, cx_peer, *z_peer.values(), *y_peer.values(), *diagonal.values(), (col, t_col, other)):
         pl.semaphore_signal(barrier, inc=1, device_id=peer, device_id_type=MESH)
 
     @pl.when(jnp.logical_not(from_self))
@@ -56,7 +57,7 @@
         pl.semaphore_signal(barrier, inc=1, device_id=(col, t_col, half), device_id_type=MESH)
 
     rows[half, col] = stage[...]
-    pl.semaphore_wait(barrier, jnp.where(from_self, 12, 13))
+    pl.semaphore_wait(barrier, jnp.where(from_self, 16, 17))
 
     def remote(src, dst, send, recv, peer):
         return pltpu.make_async_remote_copy(
@@ -103,6 +104,8 @@
         at = (0 if direction == 1 else 1, step - 1, u)
         if which == "row":
             ref, send, recv, peer = row_ref(u, -direction * behind), rr_s, rr_r, z_peer[direction * ahead]
+        elif u == 1 and step < 3:
+            ref, send, recv, peer = col_ref(0, 0), c_s, c_r, diagonal[direction * ahead]
         else:
             ref, send, recv, peer = col_ref(u, -direction * behind), c_s, c_r, y_peer[direction * ahead]
         return remote(ref, ref, send.at[at], recv.at[at], peer)
@@ -120,15 +123,12 @@
     def to_sibling(slot, u, d):
         start(remote(row_ref(u, d), row_ref(u, d), sib_s.at[slot], sib_r.at[slot], sibling))
 
-    def first_hops(which, u):
-        for step in (2, 1):
-            for direction in (1, -1):
-                start(hop(which, direction, step, u))
-
     def begin_row(u):
         if u == 1:
             arrived(row_ref(1, 0), rx_r)
-        first_hops("row", u)
+        for step in (2, 1):
+            for direction in (1, -1):
+                start(hop("row", direction, step, u))
         to_sibling(u, u, 0)
 
     def forward(which, step, u):
@@ -160,11 +160,7 @@
                 lhs[here, FRAMES + j * HALF:FRAMES + (j + 1) * HALF] = lo
                 lhs[here, 2 * FRAMES + j * HALF:2 * FRAMES + (j + 1) * HALF] = hi
 
-    def begin_col(u):
-        if u == 1:
-            arrived(col_ref(1, 0), cx_r)
-            first_hops("col", 1)
-            return
+    def begin_col():
         for g in range(2):
             arrived(traw.at[g], t_r.at[g])
         first, second = traw[0], traw[1]
@@ -173,8 +169,11 @@
         mine = col_ref(0, 0)
         mine[:, :HALF] = first - mean
         mine[:, HALF:] = second - mean
+        for step in (2, 1):
+            for u in range(2):
+                for direction in (1, -1):
+                    start(hop("col", direction, step, u))
         start(remote(mine, mine, cx_s, cx_r, cx_peer))
-        first_hops("col", 0)
 
     base = part(y)
     sign = 1 - 2 * lax.rem(base, 2)
@@ -203,28 +202,28 @@
     start(remote(row_ref(0, 0), row_ref(0, 0), rx_s, rx_r, rx_peer))
     begin_row(0)
     begin_row(1)
-    begin_col(0)
+    begin_col()
     forward("row", 2, 0)
-    begin_col(1)
+    forward("row", 1, 0)
     forward("row", 2, 1)
+    to_lhs(0, 0)
     forward("col", 2, 0)
-    forward("row", 1, 0)
-    to_lhs(0, 0)
-    to_lhs(0, 1)
     forward("col", 2, 1)
     forward("row", 1, 1)
+    to_lhs(0, 1)
     to_lhs(2, 0)
+    to_lhs(1, 0)
     forward("row", 3, 0)
     forward("row", 4, 0)
-    to_lhs(1, 0)
     to_lhs(2, 1)
     to_lhs(1, 1)
     forward("row", 3, 1)
     forward("row", 4, 1)
     to_lhs(3, 0)
     to_lhs(4, 0)
-    for u in range(2):
-        forward("col", 1, u)
+    forward("col", 1, 0)
+    forward("col", 1, 1)
+    arrived(col_ref(1, 0), cx_r)
     to_rhs((1, 2))
     multiply((1, 2), 0)
     to_lhs(3, 1)

time: 40.4 us -> 40.6 us (level); the launches traced: 39.8 us -> 40.5 us
  Pallas kernels: 37.7 us -> 38.3 us
    pallas_call x1, Pallas kernels: 37.7 us -> 38.3 us  [body(): pl.pallas_call(kernel, out_shape=jax.ShapeDtypeStruct((1024, 512), jnp.fl...]
where the time goes in v1:
time: 40.6 us; the launch traced here: 40.5 us
  Pallas kernels  38.3 us (94%)
  local copies, waits for them, and re-layouts  2.16 us (5%)
    pallas_call x1, Pallas kernels, body(): pl.pallas_call(kernel, out_shape=jax.ShapeDtypeStruct((1024, 512), jnp.fl...  38.3 us
    unnamed x3, local copies, waits for them, and re-layouts  2.16 us

profile of v1, /device:TPU:1, one launch (start us, length us, event | category | flops | bytes accessed | tf_op | source)
XLA Modules:
  0.0 40.5 jit_solution(7758025981971994010)
XLA Ops:
  0.0 0.0 copy-start
  0.0 0.8 %copy-done = f32[256,64]{0,1:T(8,128)S(1)} copy-done((f32[256,64]{0,1:T(8,128)S(1)}, f32[256,64]{0,1:T(8,128)}, u32[]{:S(2)}) %copy-start) | copy-done | bytes 65560
  0.8 38.3 %shard_map.17 = f32[1024,512]{1,0:T(8,128)S(1)} custom-call(f32[64,256]{1,0:T(8,128)S(1)} %bitcast.1), custom_call_target="tpu_custom_call" | custom-call | flops 1610612736 | bytes 2097152 | tf_op jit(solution)/shard_map/pallas_call | solution.py:249
  39.2 1.3 %copy.3 = f32[1024,512]{1,0:T(8,128)} copy(f32[1024,512]{1,0:T(8,128)S(1)} %shard_map.17) | data formatting | bytes 4194304
Async XLA Ops:
  0.0 0.8 %copy-start = (f32[256,64]{0,1:T(8,128)S(1)}, f32[256,64]{0,1:T(8,128)}, u32[]{:S(2)}) copy-start(f32[256,64]{0,1:T(8,128)} %param.1) | copy-start | bytes 196612

commit v2 on v1

--- a/solution.py
+++ b/solution.py
@@ -56,7 +56,7 @@
     def _():
         pl.semaphore_signal(barrier, inc=1, device_id=(col, t_col, half), device_id_type=MESH)
 
-    rows[half, col] = stage[...]
+    rows[half, xh, z] = stage[...]
     pl.semaphore_wait(barrier, jnp.where(from_self, 16, 17))
 
     def remote(src, dst, send, recv, peer):
@@ -90,75 +90,87 @@
 
             t_copies.append((t_self[s], far))
 
-    def k_of(u, d):
-        return (xh if u == 0 else 1 - xh) * RING + mod8(z + d)
+    signs = (1, -1)
+    distances = (0, -1, 1, -2, 2, -3, 3, 4)
 
     def row_ref(u, d):
-        return rows.at[half, k_of(u, d)]
+        return rows.at[half, xh if u == 0 else 1 - xh, mod8(z + d)]
+
+    def row_pair(d, core):
+        return rows.at[core, :, mod8(z + d)]
 
     def col_ref(u, d):
         return cols.at[part(mod8(y + d)), xl if u == 0 else 1 - xl]
+
+    def col_pair(d):
+        return cols.at[part(mod8(y + d))]
 
     def hop(which, direction, step, u):
         behind, ahead = ((0, 1), (0, 2), (2, 1), (2, 2))[step - 1]
         at = (0 if direction == 1 else 1, step - 1, u)
+        d = -direction * behind
         if which == "row":
-            ref, send, recv, peer = row_ref(u, -direction * behind), rr_s, rr_r, z_peer[direction * ahead]
+            ref = row_pair(d, half) if step == 3 else row_ref(u, d)
+            return remote(ref, ref, rr_s.at[at], rr_r.at[at], z_peer[direction * ahead])
+        peer = y_peer[direction * ahead]
+        if step == 3:
+            ref = col_pair(d)
         elif u == 1 and step < 3:
-            ref, send, recv, peer = col_ref(0, 0), c_s, c_r, diagonal[direction * ahead]
+            ref, peer = col_ref(0, 0), diagonal[direction * ahead]
         else:
-            ref, send, recv, peer = col_ref(u, -direction * behind), c_s, c_r, y_peer[direction * ahead]
-        return remote(ref, ref, send.at[at], recv.at[at], peer)
-
-    def sends(direction, step, u):
-        return step < 4 or (direction == 1) == (u == 0)
-
-    def slots(step, u):
-        if step == 0:
-            return ((u, 0),)
-        if step == 4:
-            return ((14 + u, 4),)
-        return tuple((2 + (step - 1) * 4 + (0 if n == 1 else 2) + u, -n * step) for n in (1, -1))
-
-    def to_sibling(slot, u, d):
-        start(remote(row_ref(u, d), row_ref(u, d), sib_s.at[slot], sib_r.at[slot], sibling))
+            ref = col_ref(u, d)
+        return remote(ref, ref, c_s.at[at], c_r.at[at], peer)
+
+    def to_sibling(d):
+        slot = distances.index(d)
+        start(remote(row_pair(d, half), row_pair(d, half), sib_s.at[slot], sib_r.at[slot], sibling))
 
     def begin_row(u):
         if u == 1:
             arrived(row_ref(1, 0), rx_r)
         for step in (2, 1):
-            for direction in (1, -1):
+            for direction in signs:
                 start(hop("row", direction, step, u))
-        to_sibling(u, u, 0)
-
-    def forward(which, step, u):
-        n = 0
-        for direction in (1, -1):
-            if not sends(direction, step, u):
-                continue
-            slot, d = slots(step, u)[n]
-            n += 1
-            ref, recv = (row_ref(u, d), rr_r) if which == "row" else (col_ref(u, d), c_r)
-            arrived(ref, recv.at[0 if direction == 1 else 1, step - 1, u])
-            for later in (4, 3) if step == 2 else ():
-                if sends(direction, later, u):
-                    start(hop(which, direction, later, u))
-            if which == "row":
-                to_sibling(slot, u, d)
-
-    def to_lhs(step, u):
-        for slot, d in slots(step, u):
-            k = k_of(u, d)
-            arrived(rows.at[other, k], sib_r.at[slot])
-            first, second = rows[0, k], rows[1, k]
-            total = jnp.sum(first, axis=1, keepdims=True) + jnp.sum(second, axis=1, keepdims=True)
-            mean = total / FRAMES
-            here = pl.ds(pl.multiple_of(k * 64, 64), 64)
-            for j, value in enumerate((first, second)):
-                hi, lo = split(value - mean)
-                lhs[here, j * HALF:(j + 1) * HALF] = hi
-                lhs[here, FRAMES + j * HALF:FRAMES + (j + 1) * HALF] = lo
-                lhs[here, 2 * FRAMES + j * HALF:2 * FRAMES + (j + 1) * HALF] = hi
+        if u == 1:
+            to_sibling(0)
+
+    def come(which, direction, step):
+        recv = rr_r if which == "row" else c_r
+        i = 0 if direction == 1 else 1
+        d = -direction * step
+        if step == 3:
+            arrived(row_pair(d, half) if which == "row" else col_pair(d), recv.at[i, 2, 0])
+        elif step == 4:
+            u = i
+            arrived(row_ref(u, 4) if which == "row" else col_ref(u, 4), recv.at[i, 3, u])
+        else:
+            for u in range(2):
+                arrived(row_ref(u, d) if which == "row" else col_ref(u, d), recv.at[i, step - 1, u])
+
+    def forward(which, step):
+        for direction in signs:
+            come(which, direction, step)
+            if step == 2:
+                start(hop(which, direction, 4, 0 if direction == 1 else 1))
+                start(hop(which, direction, 3, 0))
+            if which == "row" and step < 4:
+                to_sibling(-direction * step)
+        if which == "row" and step == 4:
+            to_sibling(4)
+
+    def to_lhs(*ds):
+        for d in ds:
+            arrived(row_pair(d, other), sib_r.at[distances.index(d)])
+            for x in range(2):
+                first, second = rows[0, x, mod8(z + d)], rows[1, x, mod8(z + d)]
+                total = jnp.sum(first, axis=1, keepdims=True) + jnp.sum(second, axis=1, keepdims=True)
+                mean = total / FRAMES
+                here = pl.ds(pl.multiple_of(x * 512 + mod8(z + d) * 64, 64), 64)
+                for j, value in enumerate((first, second)):
+                    hi, lo = split(value - mean)
+                    lhs[here, j * HALF:(j + 1) * HALF] = hi
+                    lhs[here, FRAMES + j * HALF:FRAMES + (j + 1) * HALF] = lo
+                    lhs[here, 2 * FRAMES + j * HALF:2 * FRAMES + (j + 1) * HALF] = hi
 
     def begin_col():
         for g in range(2):
@@ -191,7 +203,7 @@
             rhs[here, 2 * FRAMES:] = lo
 
     def multiply(steps, u):
-        here = pl.ds(pl.multiple_of((xh if u == 0 else 1 - xh) * 512, 512), 512)
+        here = pl.ds(u * 512, 512)
         product = lax.dot_general(
             lhs[here, :], rhs[...], (((1,), (1,)), ((), ())), preferred_element_type=jnp.float32)
         for i, step in enumerate(steps):
@@ -203,35 +215,22 @@
     begin_row(0)
     begin_row(1)
     begin_col()
-    forward("row", 2, 0)
-    forward("row", 1, 0)
-    forward("row", 2, 1)
-    to_lhs(0, 0)
-    forward("col", 2, 0)
-    forward("col", 2, 1)
-    forward("row", 1, 1)
-    to_lhs(0, 1)
-    to_lhs(2, 0)
-    to_lhs(1, 0)
-    forward("row", 3, 0)
-    forward("row", 4, 0)
-    to_lhs(2, 1)
-    to_lhs(1, 1)
-    forward("row", 3, 1)
-    forward("row", 4, 1)
-    to_lhs(3, 0)
-    to_lhs(4, 0)
-    forward("col", 1, 0)
-    forward("col", 1, 1)
+    forward("row", 2)
+    to_lhs(0)
+    forward("col", 2)
+    forward("row", 1)
+    to_lhs(-2, 2)
+    forward("row", 3)
+    forward("row", 4)
+    to_lhs(-1, 1)
+    forward("col", 1)
     arrived(col_ref(1, 0), cx_r)
     to_rhs((1, 2))
+    to_lhs(-3, 3, 4)
     multiply((1, 2), 0)
-    to_lhs(3, 1)
-    to_lhs(4, 1)
     multiply((1, 2), 1)
-    for u in range(2):
-        forward("col", 3, u)
-        forward("col", 4, u)
+    forward("col", 3)
+    forward("col", 4)
     to_rhs((3, 4))
     multiply((3, 4), 0)
     multiply((3, 4), 1)
@@ -253,12 +252,12 @@
         out_specs=pl.BlockSpec(memory_space=pltpu.VMEM),
         scratch_shapes=[
             pltpu.VMEM((2, 32, HALF), jnp.float32),
-            pltpu.VMEM((2, 16, 64, HALF), jnp.float32),
+            pltpu.VMEM((2, 2, 8, 64, HALF), jnp.float32),
             pltpu.VMEM((8, 2, 32, FRAMES), jnp.float32),
             pltpu.VMEM((1024, 3 * FRAMES), jnp.bfloat16),
             pltpu.VMEM((2 * TILE, 3 * FRAMES), jnp.bfloat16),
             dma((2,)), dma((2,)), dma, dma, dma, dma, dma((2, 4, 2)), dma((2, 4, 2)), dma((2, 4, 2)), dma((2, 4, 2)),
-            dma((16,)), dma((16,)),
+            dma((8,)), dma((8,)),
         ],
         compiler_params=pltpu.CompilerParams(
             collective_id=0, has_side_effects=True, vmem_limit_bytes=40 * 1024 * 1024),

time: 40.6 us -> 40.5 us (level)
  no operation moved by 1% of the time
where the time goes in v2:
time: 40.5 us; the launch traced here: 40.4 us
  Pallas kernels  38.2 us (94%)
  local copies, waits for them, and re-layouts  2.16 us (5%)
    pallas_call x1, Pallas kernels, body(): pl.pallas_call(kernel, out_shape=jax.ShapeDtypeStruct((1024, 512), jnp.fl...  38.2 us
    unnamed x3, local copies, waits for them, and re-layouts  2.16 us

profile of v2, /device:TPU:1, one launch (start us, length us, event | category | flops | bytes accessed | tf_op | source)
XLA Modules:
  0.0 40.4 jit_solution(10009455977876156666)
XLA Ops:
  0.0 0.0 copy-start
  0.0 0.8 %copy-done = f32[256,64]{0,1:T(8,128)S(1)} copy-done((f32[256,64]{0,1:T(8,128)S(1)}, f32[256,64]{0,1:T(8,128)}, u32[]{:S(2)}) %copy-start) | copy-done | bytes 65560
  0.8 38.2 %shard_map.17 = f32[1024,512]{1,0:T(8,128)S(1)} custom-call(f32[64,256]{1,0:T(8,128)S(1)} %bitcast.1), custom_call_target="tpu_custom_call" | custom-call | flops 1610612736 | bytes 2097152 | tf_op jit(solution)/shard_map/pallas_call | solution.py:248
  39.1 1.3 %copy.3 = f32[1024,512]{1,0:T(8,128)} copy(f32[1024,512]{1,0:T(8,128)S(1)} %shard_map.17) | data formatting | bytes 4194304
Async XLA Ops:
  0.0 0.8 %copy-start = (f32[256,64]{0,1:T(8,128)S(1)}, f32[256,64]{0,1:T(8,128)}, u32[]{:S(2)}) copy-start(f32[256,64]{0,1:T(8,128)} %param.1) | copy-start | bytes 196612

commit v3 on v2

--- a/solution.py
+++ b/solution.py
@@ -22,8 +22,8 @@
     return hi, lo
 
 
-def kernel(stage, out_ref, traw, rows, cols, lhs, rhs,
-           t_s, t_r, rx_s, rx_r, cx_s, cx_r, rr_s, rr_r, c_s, c_r, sib_s, sib_r):
+def kernel(x_ref, out_ref, stage, traw, rows, cols, lhs, rhs,
+           in_s, t_s, t_r, rx_s, rx_r, cx_s, cx_r, rr_s, rr_r, c_s, c_r, sib_s, sib_r):
     row = lax.axis_index("row")
     col = lax.axis_index("col")
     half = lax.axis_index("half")
@@ -31,6 +31,9 @@
     xh, z = col // RING, lax.rem(col, RING)
     other = 1 - half
 
+    fetch = pltpu.make_async_copy(x_ref, stage, in_s)
+    fetch.start()
+
     sibling = (row, col, other)
     rx_peer = (row, (1 - xh) * RING + z, half)
     z_peer = {n: (row, xh * RING + mod8(z + n), half) for n in (1, -1, 2, -2)}
@@ -56,6 +59,7 @@
     def _():
         pl.semaphore_signal(barrier, inc=1, device_id=(col, t_col, half), device_id_type=MESH)
 
+    fetch.wait()
     rows[half, xh, z] = stage[...]
     pl.semaphore_wait(barrier, jnp.where(from_self, 16, 17))
 
@@ -248,21 +252,22 @@
     return pl.pallas_call(
         kernel,
         out_shape=jax.ShapeDtypeStruct((1024, 512), jnp.float32),
-        in_specs=[pl.BlockSpec(memory_space=pltpu.VMEM)],
+        in_specs=[pl.BlockSpec(memory_space=pltpu.HBM)],
         out_specs=pl.BlockSpec(memory_space=pltpu.VMEM),
         scratch_shapes=[
+            pltpu.VMEM((64, HALF), jnp.float32),
             pltpu.VMEM((2, 32, HALF), jnp.float32),
             pltpu.VMEM((2, 2, 8, 64, HALF), jnp.float32),
             pltpu.VMEM((8, 2, 32, FRAMES), jnp.float32),
             pltpu.VMEM((1024, 3 * FRAMES), jnp.bfloat16),
             pltpu.VMEM((2 * TILE, 3 * FRAMES), jnp.bfloat16),
-            dma((2,)), dma((2,)), dma, dma, dma, dma, dma((2, 4, 2)), dma((2, 4, 2)), dma((2, 4, 2)), dma((2, 4, 2)),
+            dma, dma((2,)), dma((2,)), dma, dma, dma, dma, dma((2, 4, 2)), dma((2, 4, 2)), dma((2, 4, 2)), dma((2, 4, 2)),
             dma((8,)), dma((8,)),
         ],
         compiler_params=pltpu.CompilerParams(
             collective_id=0, has_side_effects=True, vmem_limit_bytes=40 * 1024 * 1024),
         cost_estimate=pl.CostEstimate(flops=3 * 2 * 1024 * 512 * 512, bytes_accessed=2 << 20, transcendentals=0),
-    )(frames.T)
+    )(pltpu.with_memory_space_constraint(frames.T, pltpu.HBM))
 
 
 def solution(mesh):

time: 40.5 us -> 39.7 us (0.980)
  local copies, waits for them, and re-layouts: 2.16 us -> 1.32 us
    unnamed x3 -> x1, local copies, waits for them, and re-layouts: 2.16 us -> 1.32 us
where the time goes in v3:
time: 39.7 us; the launch traced here: 39.5 us
  Pallas kernels  38.2 us (96%)
  local copies, waits for them, and re-layouts  1.32 us (3%)
    pallas_call x1, Pallas kernels, body(): pl.pallas_call(kernel, out_shape=jax.ShapeDtypeStruct((1024, 512), jnp.fl...  38.2 us
    unnamed x1, local copies, waits for them, and re-layouts  1.32 us

profile of v3, /device:TPU:1, one launch (start us, length us, event | category | flops | bytes accessed | tf_op | source)
XLA Modules:
  0.0 39.5 jit_solution(10336610555648143822)
XLA Ops:
  0.0 38.2 %shard_map.17 = f32[1024,512]{1,0:T(8,128)S(1)} custom-call(f32[64,256]{1,0:T(8,128)} %bitcast.1), custom_call_target="tpu_custom_call" | custom-call | flops 1610612736 | bytes 2097152 | tf_op jit(solution)/shard_map/pallas_call | solution.py:252
  38.2 1.3 %copy.3 = f32[1024,512]{1,0:T(8,128)} copy(f32[1024,512]{1,0:T(8,128)S(1)} %shard_map.17) | data formatting | bytes 4194304

commit v4 on v3

--- a/solution.py
+++ b/solution.py
@@ -114,7 +114,7 @@
         at = (0 if direction == 1 else 1, step - 1, u)
         d = -direction * behind
         if which == "row":
-            ref = row_pair(d, half) if step == 3 else row_ref(u, d)
+            ref = row_pair(d, half) if step in (2, 3) else row_ref(u, d)
             return remote(ref, ref, rr_s.at[at], rr_r.at[at], z_peer[direction * ahead])
         peer = y_peer[direction * ahead]
         if step == 3:
@@ -132,9 +132,9 @@
     def begin_row(u):
         if u == 1:
             arrived(row_ref(1, 0), rx_r)
-        for step in (2, 1):
+        for step in (1,) if u == 0 else (2, 1):
             for direction in signs:
-                start(hop("row", direction, step, u))
+                start(hop("row", direction, step, 0 if step == 2 else u))
         if u == 1:
             to_sibling(0)
 
@@ -142,8 +142,8 @@
         recv = rr_r if which == "row" else c_r
         i = 0 if direction == 1 else 1
         d = -direction * step
-        if step == 3:
-            arrived(row_pair(d, half) if which == "row" else col_pair(d), recv.at[i, 2, 0])
+        if step == 3 or (which == "row" and step == 2):
+            arrived(row_pair(d, half) if which == "row" else col_pair(d), recv.at[i, step - 1, 0])
         elif step == 4:
             u = i
             arrived(row_ref(u, 4) if which == "row" else col_ref(u, 4), recv.at[i, 3, u])

time: 39.7 us -> 40.8 us (1.028)
  Pallas kernels: 38.2 us -> 39.3 us
    pallas_call x1, Pallas kernels: 38.2 us -> 39.3 us  [body(): pl.pallas_call(kernel, out_shape=jax.ShapeDtypeStruct((1024, 512), jnp.fl...]
where the time goes in v4:
time: 40.8 us; the launch traced here: 40.6 us
  Pallas kernels  39.3 us (96%)
  local copies, waits for them, and re-layouts  1.32 us (3%)
    pallas_call x1, Pallas kernels, body(): pl.pallas_call(kernel, out_shape=jax.ShapeDtypeStruct((1024, 512), jnp.fl...  39.3 us
    unnamed x1, local copies, waits for them, and re-layouts  1.32 us

profile of v4, /device:TPU:1, one launch (start us, length us, event | category | flops | bytes accessed | tf_op | source)
XLA Modules:
  0.0 40.6 jit_solution(7505327906181604568)
XLA Ops:
  0.0 39.3 %shard_map.17 = f32[1024,512]{1,0:T(8,128)S(1)} custom-call(f32[64,256]{1,0:T(8,128)} %bitcast.1), custom_call_target="tpu_custom_call" | custom-call | flops 1610612736 | bytes 2097152 | tf_op jit(solution)/shard_map/pallas_call | solution.py:252
  39.3 1.3 %copy.3 = f32[1024,512]{1,0:T(8,128)} copy(f32[1024,512]{1,0:T(8,128)S(1)} %shard_map.17) | data formatting | bytes 4194304

commit v5 on v3

--- a/solution.py
+++ b/solution.py
@@ -217,8 +217,8 @@
     transpose_out()
     start(remote(row_ref(0, 0), row_ref(0, 0), rx_s, rx_r, rx_peer))
     begin_row(0)
+    begin_col()
     begin_row(1)
-    begin_col()
     forward("row", 2)
     to_lhs(0)
     forward("col", 2)

time: 39.7 us -> 41.4 us (1.043)
  the two profiles are of different devices: /device:TPU:1 before, /device:TPU:23 now
where the time goes in v5:
time: 41.4 us; the launch traced here: 41.3 us
  Pallas kernels  39.9 us (96%)
  local copies, waits for them, and re-layouts  1.32 us (3%)
    pallas_call x1, Pallas kernels, body(): pl.pallas_call(kernel, out_shape=jax.ShapeDtypeStruct((1024, 512), jnp.fl...  39.9 us
    unnamed x1, local copies, waits for them, and re-layouts  1.32 us

profile of v5, /device:TPU:23, one launch (start us, length us, event | category | flops | bytes accessed | tf_op | source)
XLA Modules:
  0.0 41.3 jit_solution(7413472418060808321)
XLA Ops:
  0.0 39.9 %shard_map.17 = f32[1024,512]{1,0:T(8,128)S(1)} custom-call(f32[64,256]{1,0:T(8,128)} %bitcast.1), custom_call_target="tpu_custom_call" | custom-call | flops 1610612736 | bytes 2097152 | tf_op jit(solution)/shard_map/pallas_call | solution.py:252
  39.9 1.3 %copy.3 = f32[1024,512]{1,0:T(8,128)} copy(f32[1024,512]{1,0:T(8,128)S(1)} %shard_map.17) | data formatting | bytes 4194304

commit v6 on v3

--- a/solution.py
+++ b/solution.py
@@ -220,8 +220,8 @@
     begin_row(1)
     begin_col()
     forward("row", 2)
+    forward("col", 2)
     to_lhs(0)
-    forward("col", 2)
     forward("row", 1)
     to_lhs(-2, 2)
     forward("row", 3)

time: 39.7 us -> 39.7 us (level)
  no operation moved by 1% of the time
where the time goes in v6:
time: 39.7 us; the launch traced here: 39.5 us
  Pallas kernels  38.2 us (96%)
  local copies, waits for them, and re-layouts  1.32 us (3%)
    pallas_call x1, Pallas kernels, body(): pl.pallas_call(kernel, out_shape=jax.ShapeDtypeStruct((1024, 512), jnp.fl...  38.2 us
    unnamed x1, local copies, waits for them, and re-layouts  1.32 us

profile of v6, /device:TPU:1, one launch (start us, length us, event | category | flops | bytes accessed | tf_op | source)
XLA Modules:
  0.0 39.5 jit_solution(13268615768836014196)
XLA Ops:
  0.0 38.2 %shard_map.17 = f32[1024,512]{1,0:T(8,128)S(1)} custom-call(f32[64,256]{1,0:T(8,128)} %bitcast.1), custom_call_target="tpu_custom_call" | custom-call | flops 1610612736 | bytes 2097152 | tf_op jit(solution)/shard_map/pallas_call | solution.py:252
  38.2 1.3 %copy.3 = f32[1024,512]{1,0:T(8,128)} copy(f32[1024,512]{1,0:T(8,128)S(1)} %shard_map.17) | data formatting | bytes 4194304

commit v7 on v3

--- a/solution.py
+++ b/solution.py
@@ -206,8 +206,8 @@
             rhs[here, FRAMES:2 * FRAMES] = hi
             rhs[here, 2 * FRAMES:] = lo
 
-    def multiply(steps, u):
-        here = pl.ds(u * 512, 512)
+    def multiply(steps, m):
+        here = pl.ds(m * 256, 256)
         product = lax.dot_general(
             lhs[here, :], rhs[...], (((1,), (1,)), ((), ())), preferred_element_type=jnp.float32)
         for i, step in enumerate(steps):
@@ -231,13 +231,13 @@
     arrived(col_ref(1, 0), cx_r)
     to_rhs((1, 2))
     to_lhs(-3, 3, 4)
-    multiply((1, 2), 0)
-    multiply((1, 2), 1)
+    for m in range(4):
+        multiply((1, 2), m)
     forward("col", 3)
     forward("col", 4)
     to_rhs((3, 4))
-    multiply((3, 4), 0)
-    multiply((3, 4), 1)
+    for m in range(4):
+        multiply((3, 4), m)
 
     for copy in pending:
         copy.wait_send()

time: 39.7 us -> 39.7 us (level)
  no operation moved by 1% of the time
where the time goes in v7:
time: 39.7 us; the launch traced here: 39.5 us
  Pallas kernels  38.2 us (96%)
  local copies, waits for them, and re-layouts  1.32 us (3%)
    pallas_call x1, Pallas kernels, body(): pl.pallas_call(kernel, out_shape=jax.ShapeDtypeStruct((1024, 512), jnp.fl...  38.2 us
    unnamed x1, local copies, waits for them, and re-layouts  1.32 us

profile of v7, /device:TPU:1, one launch (start us, length us, event | category | flops | bytes accessed | tf_op | source)
XLA Modules:
  0.0 39.5 jit_solution(5469472133107934728)
XLA Ops:
  0.0 38.2 %shard_map.17 = f32[1024,512]{1,0:T(8,128)S(1)} custom-call(f32[64,256]{1,0:T(8,128)} %bitcast.1), custom_call_target="tpu_custom_call" | custom-call | flops 1610612736 | bytes 2097152 | tf_op jit(solution)/shard_map/pallas_call | solution.py:252
  38.2 1.3 %copy.3 = f32[1024,512]{1,0:T(8,128)} copy(f32[1024,512]{1,0:T(8,128)S(1)} %shard_map.17) | data formatting | bytes 4194304
